TPU v7x, 512 devices: a whole 4x4x16 slice. The times are simulated.
512 devices in a mesh: net: 64 (over z, x), scen: 8 (over y, core).
Axes of the slice: x: 4, y: 4, z: 16, core: 2. Of those that a mesh axis runs over, the one named last changes fastest.
Arguments:
- device_group: int32 [64], replicated, may hold values from 3 to 63, as said below
- column_blocks: int32 [256, 12], P('net'), may hold values from 0 to 255, as said below
- impedance_real: bfloat16 [256, 12, 128, 128], P('net'), may hold values from 0 to 0.015258789
- impedance_imag: bfloat16 [256, 12, 128, 128], P('net'), may hold values from 0 to 0.0076293945
- building_phase: int32 [65536], P('net'), may hold values from 0 to 32767, as said below
- building_power: float32 [65536], P('net'), may hold values from 0.2 to 1
- reactive_ratio: float32 [65536], P('net'), may hold values from 0.1 to 0.8
- copula_normals: float32 [65536, 1024], P('net', 'scen'), may hold values from -6 to 6
- source_angle: float32 [32768], P('net'), may hold values from -3.140625 to 3.140625
Outputs:
- voltage_real: float32 [32768, 1024], P('net', 'scen')
- voltage_imag: float32 [32768, 1024], P('net', 'scen')
- drop_mean: float32 [32768, 16], P('net')
Inputs may be any that keep to these rules, and one draw needn't show every extreme that they name: `device_group`: never falling along the devices; each group is a run of 1 to 4 consecutive devices and is labelled by the index of its last device; the first 4 devices form one group. `column_blocks`: slot 0 of block row r is r itself; the first min(12, 4 times the devices of r's group) slots are distinct blocks of devices of r's group; the other slots repeat r. `building_phase`: building b feeds a phase of the device that holds b: from 512 * (b // 1024) to that plus 512 - 1; every phase is fed by at least one building.
All inputs are finite; a program needn't handle non-finite values.
Results may differ from a plain program's by a relative error of at most 0.0063.
Values may be sent and summed in bfloat16 or wider, within the bound.
No kernel may reach another device: no remote copies, remote signals or barrier semaphores. Data moves between devices by JAX's collectives and lax.ppermute only.
A program may use at most 64 MiB of HBM per device.

v0:
```python
import jax
import jax.numpy as jnp
from jax import lax
from jax.sharding import PartitionSpec as P

GMAX = 4
ITERS = 3
TIMES = 16
floor_square = 0.49


def from_behind(value, axis, steps):
    count = lax.axis_size(axis)
    leading, last = (max(0, -steps), min(count, count - steps))
    return lax.ppermute(value, axis, [(source, source + steps) for source in range(leading, last)])


def shards(
    device_group,
    column_blocks,
    impedance_real,
    impedance_imag,
    building_phase,
    building_power,
    reactive_ratio,
    copula_normals,
    source_angle,
):
    block_count, slot_count, block_width, other_width = impedance_real.shape
    phase_count = block_count * block_width
    column_count = copula_normals.shape[1]
    local_scen = column_count // TIMES
    total_scen = local_scen * lax.axis_size("scen")
    scenario = (
        lax.axis_index("scen") * local_scen + jnp.arange(column_count, dtype=jnp.int32) // TIMES
    ).astype(jnp.float32)
    scen_level = 0.5 + scenario / (total_scen - 1)
    real_power = (
        building_power[:, None] * scen_level[None, :] * jnp.exp(0.4 * copula_normals - 0.08)
    )
    both_power = jnp.concatenate([real_power, real_power * reactive_ratio[:, None]], axis=1)
    net_index = lax.axis_index("net")
    local_phase = building_phase - net_index * phase_count
    loads = jax.ops.segment_sum(both_power, local_phase, num_segments=phase_count)
    load_real = loads[:, :column_count]
    load_reactive = loads[:, column_count:]
    source_real = jnp.broadcast_to(jnp.cos(source_angle)[:, None], (phase_count, column_count))
    source_imag = jnp.broadcast_to(jnp.sin(source_angle)[:, None], (phase_count, column_count))
    own_group = device_group[net_index]
    group_size = jnp.sum((device_group == own_group).astype(jnp.int32))
    live_count = jnp.minimum(slot_count, group_size * block_count)
    live_slots = jnp.arange(slot_count, dtype=jnp.int32) < live_count
    owner_device = column_blocks // block_count
    window_index = (
        owner_device - net_index + (GMAX - 1)
    ) * block_count + column_blocks % block_count
    volt_real = source_real
    volt_imag = source_imag
    for sweep in range(ITERS):
        mag_square = jnp.maximum(volt_real * volt_real + volt_imag * volt_imag, floor_square)
        current_real = (load_real * volt_real + load_reactive * volt_imag) / mag_square
        current_imag = (load_real * volt_imag - load_reactive * volt_real) / mag_square
        currents = jnp.concatenate([current_real, current_imag], axis=1).astype(jnp.bfloat16)
        lower_parts = []
        upper_parts = []
        for distance in range(1, GMAX):
            lower_parts.append(from_behind(currents, "net", distance))
            upper_parts.append(from_behind(currents, "net", -distance))
        nearby = jnp.concatenate(lower_parts[::-1] + [currents] + upper_parts, axis=0).reshape(
            -1, block_width, 2 * column_count
        )
        gathered = jnp.take(nearby, window_index, axis=0)
        gathered = jnp.where(live_slots[None, :, None, None], gathered, jnp.zeros((), jnp.bfloat16))
        real_part = jnp.einsum(
            "bsij,bsjk->bik", impedance_real, gathered, preferred_element_type=jnp.float32
        ).reshape(phase_count, 2 * column_count)
        imag_part = jnp.einsum(
            "bsij,bsjk->bik", impedance_imag, gathered, preferred_element_type=jnp.float32
        ).reshape(phase_count, 2 * column_count)
        drop_real = real_part[:, :column_count] - imag_part[:, column_count:]
        drop_imag = real_part[:, column_count:] + imag_part[:, :column_count]
        volt_real = source_real - drop_real
        volt_imag = source_imag - drop_imag
    magnitude = jnp.sqrt(volt_real * volt_real + volt_imag * volt_imag)
    local_sum = jnp.sum(magnitude.reshape(phase_count, local_scen, TIMES), axis=1)
    scen_total = lax.psum(local_sum, "scen")
    drop_mean = 100.0 * (1.0 - scen_total / total_scen)
    return (volt_real, volt_imag, drop_mean)


def solution(mesh):
    in_specs = (
        P(),
        P("net", None),
        P("net", None, None, None),
        P("net", None, None, None),
        P("net"),
        P("net"),
        P("net"),
        P("net", "scen"),
        P("net"),
    )
    out_specs = (P("net", "scen"), P("net", "scen"), P("net", None))
    return jax.shard_map(shards, mesh=mesh, in_specs=in_specs, out_specs=out_specs, check_vma=False)
```

profile of v0, /device:TPU:224, one launch (start us, length us, event | category | flops | bytes accessed | tf_op | source)
XLA Modules:
  0.0 170.0 jit_solution(13973513056029608391)
XLA Ops:
  3.6 6.2 %scatter_custom_fusion = f32[512,256]{1,0:T(8,128)S(1)} fusion(s32[1024]{0:T(1024)S(1)} %broadcast_subtract_fusion, f32[1024,128]{1,0:T(8,128)S(1)} %get-tuple-element.12, f32[]{:T(128)} %constant.112, f32[1024,128]{1,0:T(8,128)S(1)} %get-tuple-element.13, f32[]{:T(128)} %constant.78.clone.1), kind=kCustom, calls=%fused_computation.7 | custom fusion | flops 524288 | bytes 1572872 | tf_op jit(solution)/shard_map/scatter-add | solution.py:44
  10.2 4.7 %collective-permute-start = (bf16[512,256]{1,0:T(8,128)(2,1)S(1)}, bf16[512,256]{1,0:T(8,128)(2,1)}, u32[]{:S(2)}, u32[]{:S(2)}) collective-permute-start(bf16[512,256]{1,0:T(8,128)(2,1)S(1)} %pad_maximum_fusion), channel_id=1, source_target_pairs={{0,24},{8,32},{16,40},{24,48},{32,56},{40,64},{48,72},{56,80},{64,... | collective-permute-start | bytes 786440 | tf_op jit(solution)/shard_map/ppermute | solution.py:15
  14.9 5.3 %collective-permute-start.1 = (bf16[512,256]{1,0:T(8,128)(2,1)S(1)}, bf16[512,256]{1,0:T(8,128)(2,1)}, u32[]{:S(2)}, u32[]{:S(2)}) collective-permute-start(bf16[512,256]{1,0:T(8,128)(2,1)S(1)} %pad_maximum_fusion), channel_id=1, source_target_pairs={{0,16},{8,24},{16,32},{24,40},{32,48},{40,56},{48,64},{56,72},{64,... | collective-permute-start | bytes 786440 | tf_op jit(solution)/shard_map/ppermute | solution.py:15
  20.1 2.8 %collective-permute-start.2 = (bf16[512,256]{1,0:T(8,128)(2,1)S(1)}, bf16[512,256]{1,0:T(8,128)(2,1)S(1)}, u32[]{:S(2)}, u32[]{:S(2)}) collective-permute-start(bf16[512,256]{1,0:T(8,128)(2,1)S(1)} %pad_maximum_fusion), channel_id=1, source_target_pairs={{0,8},{8,16},{16,24},{24,32},{32,40},{40,48},{48,56},{56,64},{64,7... | collective-permute-start | bytes 786440 | tf_op jit(solution)/shard_map/ppermute | solution.py:15
  22.9 5.2 %collective-permute-start.3 = (bf16[512,256]{1,0:T(8,128)(2,1)S(1)}, bf16[512,256]{1,0:T(8,128)(2,1)S(1)}, u32[]{:S(2)}, u32[]{:S(2)}) collective-permute-start(bf16[512,256]{1,0:T(8,128)(2,1)S(1)} %pad_maximum_fusion), channel_id=1, source_target_pairs={{8,0},{16,8},{24,16},{32,24},{40,32},{48,40},{56,48},{64,56},{72,6... | collective-permute-start | bytes 786440 | tf_op jit(solution)/shard_map/ppermute | solution.py:15
  28.1 1.9 %collective-permute-start.4 = (bf16[512,256]{1,0:T(8,128)(2,1)S(1)}, bf16[512,256]{1,0:T(8,128)(2,1)S(1)}, u32[]{:S(2)}, u32[]{:S(2)}) collective-permute-start(bf16[512,256]{1,0:T(8,128)(2,1)S(1)} %pad_maximum_fusion), channel_id=1, source_target_pairs={{16,0},{24,8},{32,16},{40,24},{48,32},{56,40},{64,48},{72,56},{80,... | collective-permute-start | bytes 786440 | tf_op jit(solution)/shard_map/ppermute | solution.py:15
  32.7 1.9 %collective-permute-start.5 = (bf16[512,256]{1,0:T(8,128)(2,1)S(1)}, bf16[512,256]{1,0:T(8,128)(2,1)S(1)}, u32[]{:S(2)}, u32[]{:S(2)}) collective-permute-start(bf16[512,256]{1,0:T(8,128)(2,1)S(1)} %pad_maximum_fusion), channel_id=1, source_target_pairs={{24,0},{32,8},{40,16},{48,24},{56,32},{64,40},{72,48},{80,56},{88,... | collective-permute-start | bytes 786440 | tf_op jit(solution)/shard_map/ppermute | solution.py:15
  40.2 5.0 %collective-permute-done.4 = bf16[512,256]{1,0:T(8,128)(2,1)S(1)} collective-permute-done((bf16[512,256]{1,0:T(8,128)(2,1)S(1)}, bf16[512,256]{1,0:T(8,128)(2,1)S(1)}, u32[]{:S(2)}, u32[]{:S(2)}) %collective-permute-start.4) | collective-permute-done | bytes 262176 | tf_op jit(solution)/shard_map/ppermute | solution.py:15
  46.7 4.0 %gather_fusion = bf16[48,128,256]{2,1,0:T(8,128)(2,1)} fusion(bf16[28,128,256]{2,1,0:T(8,128)(2,1)} %bitcast.1, s32[1024]{0:T(1024)S(1)} %pad_clamp_fusion), kind=kCustom, calls=%fused_computation.clone | custom fusion | bytes 6291648 | tf_op jit(solution)/shard_map/jit(_take)/gather | solution.py:72
  50.7 2.8 %fusion.4 = f32[4,256,128,1]{1,2,3,0:T(8,128)S(1)} fusion(bf16[4,12,128,128]{3,2,1,0:T(8,128)(2,1)S(1)} %copy-done, bf16[4,12,128,256]{3,2,1,0:T(8,128)(2,1)} %bitcast.53, pred[12]{0:T(512)(128)(4,1)S(1)} %iota_compare_fusion, pred[4,12]{1,0:T(4,128)(4,1)S(1)} %get-tuple-element.10), kind=kOutput, calls=%fused_computation.11 | convolution fusion | flops 405798912 | bytes 5242940 | tf_op jit(solution)/shard_map/bsij,bsjk->bik/dot_general | solution.py:74
  57.0 10.6 %collective-permute-start.7 = (bf16[512,256]{1,0:T(8,128)(2,1)S(1)}, bf16[512,256]{1,0:T(8,128)(2,1)S(1)}, u32[]{:S(2)}, u32[]{:S(2)}) collective-permute-start(bf16[512,256]{1,0:T(8,128)(2,1)S(1)} %pad_maximum_fusion.1), channel_id=1, source_target_pairs={{0,16},{8,24},{16,32},{24,40},{32,48},{40,56},{48,64},{56,72},{64,... | collective-permute-start | bytes 786440 | tf_op jit(solution)/shard_map/ppermute | solution.py:15
  69.5 6.0 %collective-permute-start.9 = (bf16[512,256]{1,0:T(8,128)(2,1)S(1)}, bf16[512,256]{1,0:T(8,128)(2,1)S(1)}, u32[]{:S(2)}, u32[]{:S(2)}) collective-permute-start(bf16[512,256]{1,0:T(8,128)(2,1)S(1)} %pad_maximum_fusion.1), channel_id=1, source_target_pairs={{8,0},{16,8},{24,16},{32,24},{40,32},{48,40},{56,48},{64,56},{72,6... | collective-permute-start | bytes 786440 | tf_op jit(solution)/shard_map/ppermute | solution.py:15
  83.1 7.1 %collective-permute-done.10 = bf16[512,256]{1,0:T(8,128)(2,1)S(1)} collective-permute-done((bf16[512,256]{1,0:T(8,128)(2,1)S(1)}, bf16[512,256]{1,0:T(8,128)(2,1)S(1)}, u32[]{:S(2)}, u32[]{:S(2)}) %collective-permute-start.10) | collective-permute-done | bytes 262176 | tf_op jit(solution)/shard_map/ppermute | solution.py:15
  91.7 4.0 %gather_fusion.1 = bf16[48,128,256]{2,1,0:T(8,128)(2,1)} fusion(bf16[28,128,256]{2,1,0:T(8,128)(2,1)} %bitcast.15, s32[1024]{0:T(1024)S(1)} %pad_clamp_fusion), kind=kCustom, calls=%fused_computation.1.clone | custom fusion | bytes 6291648 | tf_op jit(solution)/shard_map/jit(_take)/gather | solution.py:72
  95.7 2.8 %fusion.6 = f32[4,256,128,1]{1,2,3,0:T(8,128)S(1)} fusion(bf16[4,12,128,128]{3,2,1,0:T(8,128)(2,1)S(1)} %copy-done, bf16[4,12,128,256]{3,2,1,0:T(8,128)(2,1)} %bitcast.55, pred[12]{0:T(512)(128)(4,1)S(1)} %iota_compare_fusion, pred[4,12]{1,0:T(4,128)(4,1)S(1)} %get-tuple-element.10), kind=kOutput, calls=%fused_computation.13 | convolution fusion | flops 405798912 | bytes 5242940 | tf_op jit(solution)/shard_map/bsij,bsjk->bik/dot_general | solution.py:74
  102.0 5.8 %collective-permute-start.13 = (bf16[512,256]{1,0:T(8,128)(2,1)S(1)}, bf16[512,256]{1,0:T(8,128)(2,1)S(1)}, u32[]{:S(2)}, u32[]{:S(2)}) collective-permute-start(bf16[512,256]{1,0:T(8,128)(2,1)S(1)} %pad_maximum_fusion.2), channel_id=1, source_target_pairs={{0,16},{8,24},{16,32},{24,40},{32,48},{40,56},{48,64},{56,72},{64,... | collective-permute-start | bytes 786440 | tf_op jit(solution)/shard_map/ppermute | solution.py:15
  107.8 3.5 %collective-permute-start.14 = (bf16[512,256]{1,0:T(8,128)(2,1)S(1)}, bf16[512,256]{1,0:T(8,128)(2,1)S(1)}, u32[]{:S(2)}, u32[]{:S(2)}) collective-permute-start(bf16[512,256]{1,0:T(8,128)(2,1)S(1)} %pad_maximum_fusion.2), channel_id=1, source_target_pairs={{0,8},{8,16},{16,24},{24,32},{32,40},{40,48},{48,56},{56,64},{64,7... | collective-permute-start | bytes 786440 | tf_op jit(solution)/shard_map/ppermute | solution.py:15
  111.3 5.5 %collective-permute-start.15 = (bf16[512,256]{1,0:T(8,128)(2,1)S(1)}, bf16[512,256]{1,0:T(8,128)(2,1)S(1)}, u32[]{:S(2)}, u32[]{:S(2)}) collective-permute-start(bf16[512,256]{1,0:T(8,128)(2,1)S(1)} %pad_maximum_fusion.2), channel_id=1, source_target_pairs={{8,0},{16,8},{24,16},{32,24},{40,32},{48,40},{56,48},{64,56},{72,6... | collective-permute-start | bytes 786440 | tf_op jit(solution)/shard_map/ppermute | solution.py:15
  116.8 3.4 %collective-permute-start.16 = (bf16[512,256]{1,0:T(8,128)(2,1)S(1)}, bf16[512,256]{1,0:T(8,128)(2,1)S(1)}, u32[]{:S(2)}, u32[]{:S(2)}) collective-permute-start(bf16[512,256]{1,0:T(8,128)(2,1)S(1)} %pad_maximum_fusion.2), channel_id=1, source_target_pairs={{16,0},{24,8},{32,16},{40,24},{48,32},{56,40},{64,48},{72,56},{80,... | collective-permute-start | bytes 786440 | tf_op jit(solution)/shard_map/ppermute | solution.py:15
  122.2 4.5 %collective-permute-done.14 = bf16[512,256]{1,0:T(8,128)(2,1)S(1)} collective-permute-done((bf16[512,256]{1,0:T(8,128)(2,1)S(1)}, bf16[512,256]{1,0:T(8,128)(2,1)S(1)}, u32[]{:S(2)}, u32[]{:S(2)}) %collective-permute-start.14) | collective-permute-done | bytes 262176 | tf_op jit(solution)/shard_map/ppermute | solution.py:15
  126.7 7.5 %collective-permute-done.16 = bf16[512,256]{1,0:T(8,128)(2,1)S(1)} collective-permute-done((bf16[512,256]{1,0:T(8,128)(2,1)S(1)}, bf16[512,256]{1,0:T(8,128)(2,1)S(1)}, u32[]{:S(2)}, u32[]{:S(2)}) %collective-permute-start.16) | collective-permute-done | bytes 262176 | tf_op jit(solution)/shard_map/ppermute | solution.py:15
  135.8 2.5 %gather_fusion.2 = bf16[48,128,256]{2,1,0:T(8,128)(2,1)} fusion(bf16[28,128,256]{2,1,0:T(8,128)(2,1)S(1)} %bitcast.50, s32[1024]{0:T(1024)S(1)} %pad_clamp_fusion), kind=kCustom, calls=%fused_computation.2.clone | custom fusion | bytes 6291648 | tf_op jit(solution)/shard_map/jit(_take)/gather | solution.py:72
  138.3 2.8 %fusion.8 = f32[4,256,128,1]{1,2,3,0:T(8,128)S(1)} fusion(bf16[4,12,128,128]{3,2,1,0:T(8,128)(2,1)S(1)} %copy-done, bf16[4,12,128,256]{3,2,1,0:T(8,128)(2,1)} %bitcast.51, pred[12]{0:T(512)(128)(4,1)S(1)} %iota_compare_fusion, pred[4,12]{1,0:T(4,128)(4,1)S(1)} %get-tuple-element.10), kind=kOutput, calls=%fused_computation.15 | convolution fusion | flops 405798912 | bytes 5242940 | tf_op jit(solution)/shard_map/bsij,bsjk->bik/dot_general | solution.py:74
  143.6 25.8 %psum.7 = f32[512,16]{0,1:T(8,128)S(1)} all-reduce(f32[512,16]{0,1:T(8,128)S(1)} %reduce_sum.19), channel_id=1, replica_groups=mesh['net'=64,'scen'=8] {'scen'}, use_global_device_ids=true, to_apply=%region_3.5 | all-reduce | flops 8192 | bytes 65536 | tf_op jit(solution)/shard_map/psum | solution.py:86
  (83 shorter events, 36.6 us)
Async XLA Ops:
  0.6 50.0 %copy-start = (bf16[4,12,128,128]{3,2,1,0:T(8,128)(2,1)S(1)}, bf16[4,12,128,128]{3,2,1,0:T(8,128)(2,1)}, u32[]{:S(2)}) copy-start(bf16[4,12,128,128]{3,2,1,0:T(8,128)(2,1)} %param.13) | copy-start | bytes 4718596
  3.6 26.5 %copy-start.4 = (s32[4,12]{1,0:T(4,128)S(1)}, s32[4,12]{1,0:T(4,128)}, u32[]{:S(2)}) copy-start(s32[4,12]{1,0:T(4,128)} %param.12) | copy-start | bytes 580
  3.6 26.6 %copy-start.8 = (s32[64]{0:T(128)S(1)}, s32[64]{0:T(128)}, u32[]{:S(2)}) copy-start(s32[64]{0:T(128)} %param.11) | copy-start | bytes 772
  10.2 22.5 %collective-permute-start = (bf16[512,256]{1,0:T(8,128)(2,1)S(1)}, bf16[512,256]{1,0:T(8,128)(2,1)}, u32[]{:S(2)}, u32[]{:S(2)}) collective-permute-start(bf16[512,256]{1,0:T(8,128)(2,1)S(1)} %pad_maximum_fusion), channel_id=1, source_target_pairs={{0,24},{8,32},{16,40},{24,48},{32,56},{40,64},{48,72},{56,80},{64,... | collective-permute-start | bytes 786440 | tf_op jit(solution)/shard_map/ppermute | solution.py:15
  14.9 21.4 %collective-permute-start.1 = (bf16[512,256]{1,0:T(8,128)(2,1)S(1)}, bf16[512,256]{1,0:T(8,128)(2,1)}, u32[]{:S(2)}, u32[]{:S(2)}) collective-permute-start(bf16[512,256]{1,0:T(8,128)(2,1)S(1)} %pad_maximum_fusion), channel_id=1, source_target_pairs={{0,16},{8,24},{16,32},{24,40},{32,48},{40,56},{48,64},{56,72},{64,... | collective-permute-start | bytes 786440 | tf_op jit(solution)/shard_map/ppermute | solution.py:15
  20.1 17.8 %collective-permute-start.2 = (bf16[512,256]{1,0:T(8,128)(2,1)S(1)}, bf16[512,256]{1,0:T(8,128)(2,1)S(1)}, u32[]{:S(2)}, u32[]{:S(2)}) collective-permute-start(bf16[512,256]{1,0:T(8,128)(2,1)S(1)} %pad_maximum_fusion), channel_id=1, source_target_pairs={{0,8},{8,16},{16,24},{24,32},{32,40},{40,48},{48,56},{56,64},{64,7... | collective-permute-start | bytes 786440 | tf_op jit(solution)/shard_map/ppermute | solution.py:15
  22.9 16.5 %collective-permute-start.3 = (bf16[512,256]{1,0:T(8,128)(2,1)S(1)}, bf16[512,256]{1,0:T(8,128)(2,1)S(1)}, u32[]{:S(2)}, u32[]{:S(2)}) collective-permute-start(bf16[512,256]{1,0:T(8,128)(2,1)S(1)} %pad_maximum_fusion), channel_id=1, source_target_pairs={{8,0},{16,8},{24,16},{32,24},{40,32},{48,40},{56,48},{64,56},{72,6... | collective-permute-start | bytes 786440 | tf_op jit(solution)/shard_map/ppermute | solution.py:15
  28.1 17.1 %collective-permute-start.4 = (bf16[512,256]{1,0:T(8,128)(2,1)S(1)}, bf16[512,256]{1,0:T(8,128)(2,1)S(1)}, u32[]{:S(2)}, u32[]{:S(2)}) collective-permute-start(bf16[512,256]{1,0:T(8,128)(2,1)S(1)} %pad_maximum_fusion), channel_id=1, source_target_pairs={{16,0},{24,8},{32,16},{40,24},{48,32},{56,40},{64,48},{72,56},{80,... | collective-permute-start | bytes 786440 | tf_op jit(solution)/shard_map/ppermute | solution.py:15
  32.7 13.2 %collective-permute-start.5 = (bf16[512,256]{1,0:T(8,128)(2,1)S(1)}, bf16[512,256]{1,0:T(8,128)(2,1)S(1)}, u32[]{:S(2)}, u32[]{:S(2)}) collective-permute-start(bf16[512,256]{1,0:T(8,128)(2,1)S(1)} %pad_maximum_fusion), channel_id=1, source_target_pairs={{24,0},{32,8},{40,16},{48,24},{56,32},{64,40},{72,48},{80,56},{88,... | collective-permute-start | bytes 786440 | tf_op jit(solution)/shard_map/ppermute | solution.py:15
  50.7 3.3 %copy-start.5 = (bf16[4,12,128,128]{3,2,1,0:T(8,128)(2,1)S(1)}, bf16[4,12,128,128]{3,2,1,0:T(8,128)(2,1)}, u32[]{:S(2)}) copy-start(bf16[4,12,128,128]{3,2,1,0:T(8,128)(2,1)} %param.14) | copy-start | bytes 4718596
  55.0 22.4 %collective-permute-start.6 = (bf16[512,256]{1,0:T(8,128)(2,1)S(1)}, bf16[512,256]{1,0:T(8,128)(2,1)S(1)}, u32[]{:S(2)}, u32[]{:S(2)}) collective-permute-start(bf16[512,256]{1,0:T(8,128)(2,1)S(1)} %pad_maximum_fusion.1), channel_id=1, source_target_pairs={{0,24},{8,32},{16,40},{24,48},{32,56},{40,64},{48,72},{56,80},{64,... | collective-permute-start | bytes 786440 | tf_op jit(solution)/shard_map/ppermute | solution.py:15
  57.0 23.1 %collective-permute-start.7 = (bf16[512,256]{1,0:T(8,128)(2,1)S(1)}, bf16[512,256]{1,0:T(8,128)(2,1)S(1)}, u32[]{:S(2)}, u32[]{:S(2)}) collective-permute-start(bf16[512,256]{1,0:T(8,128)(2,1)S(1)} %pad_maximum_fusion.1), channel_id=1, source_target_pairs={{0,16},{8,24},{16,32},{24,40},{32,48},{40,56},{48,64},{56,72},{64,... | collective-permute-start | bytes 786440 | tf_op jit(solution)/shard_map/ppermute | solution.py:15
  67.6 13.3 %collective-permute-start.8 = (bf16[512,256]{1,0:T(8,128)(2,1)S(1)}, bf16[512,256]{1,0:T(8,128)(2,1)S(1)}, u32[]{:S(2)}, u32[]{:S(2)}) collective-permute-start(bf16[512,256]{1,0:T(8,128)(2,1)S(1)} %pad_maximum_fusion.1), channel_id=1, source_target_pairs={{0,8},{8,16},{16,24},{24,32},{32,40},{40,48},{48,56},{56,64},{64,7... | collective-permute-start | bytes 786440 | tf_op jit(solution)/shard_map/ppermute | solution.py:15
  69.5 12.8 %collective-permute-start.9 = (bf16[512,256]{1,0:T(8,128)(2,1)S(1)}, bf16[512,256]{1,0:T(8,128)(2,1)S(1)}, u32[]{:S(2)}, u32[]{:S(2)}) collective-permute-start(bf16[512,256]{1,0:T(8,128)(2,1)S(1)} %pad_maximum_fusion.1), channel_id=1, source_target_pairs={{8,0},{16,8},{24,16},{32,24},{40,32},{48,40},{56,48},{64,56},{72,6... | collective-permute-start | bytes 786440 | tf_op jit(solution)/shard_map/ppermute | solution.py:15
  75.5 14.6 %collective-permute-start.10 = (bf16[512,256]{1,0:T(8,128)(2,1)S(1)}, bf16[512,256]{1,0:T(8,128)(2,1)S(1)}, u32[]{:S(2)}, u32[]{:S(2)}) collective-permute-start(bf16[512,256]{1,0:T(8,128)(2,1)S(1)} %pad_maximum_fusion.1), channel_id=1, source_target_pairs={{16,0},{24,8},{32,16},{40,24},{48,32},{56,40},{64,48},{72,56},{80,... | collective-permute-start | bytes 786440 | tf_op jit(solution)/shard_map/ppermute | solution.py:15
  77.5 13.5 %collective-permute-start.11 = (bf16[512,256]{1,0:T(8,128)(2,1)S(1)}, bf16[512,256]{1,0:T(8,128)(2,1)S(1)}, u32[]{:S(2)}, u32[]{:S(2)}) collective-permute-start(bf16[512,256]{1,0:T(8,128)(2,1)S(1)} %pad_maximum_fusion.1), channel_id=1, source_target_pairs={{24,0},{32,8},{40,16},{48,24},{56,32},{64,40},{72,48},{80,56},{88,... | collective-permute-start | bytes 786440 | tf_op jit(solution)/shard_map/ppermute | solution.py:15
  95.7 3.3 %copy-start.6 = (bf16[4,12,128,128]{3,2,1,0:T(8,128)(2,1)S(1)}, bf16[4,12,128,128]{3,2,1,0:T(8,128)(2,1)}, u32[]{:S(2)}) copy-start(bf16[4,12,128,128]{3,2,1,0:T(8,128)(2,1)} %param.14) | copy-start | bytes 4718596
  100.1 20.1 %collective-permute-start.12 = (bf16[512,256]{1,0:T(8,128)(2,1)S(1)}, bf16[512,256]{1,0:T(8,128)(2,1)S(1)}, u32[]{:S(2)}, u32[]{:S(2)}) collective-permute-start(bf16[512,256]{1,0:T(8,128)(2,1)S(1)} %pad_maximum_fusion.2), channel_id=1, source_target_pairs={{0,24},{8,32},{16,40},{24,48},{32,56},{40,64},{48,72},{56,80},{64,... | collective-permute-start | bytes 786440 | tf_op jit(solution)/shard_map/ppermute | solution.py:15
  102.0 20.2 %collective-permute-start.13 = (bf16[512,256]{1,0:T(8,128)(2,1)S(1)}, bf16[512,256]{1,0:T(8,128)(2,1)S(1)}, u32[]{:S(2)}, u32[]{:S(2)}) collective-permute-start(bf16[512,256]{1,0:T(8,128)(2,1)S(1)} %pad_maximum_fusion.2), channel_id=1, source_target_pairs={{0,16},{8,24},{16,32},{24,40},{32,48},{40,56},{48,64},{56,72},{64,... | collective-permute-start | bytes 786440 | tf_op jit(solution)/shard_map/ppermute | solution.py:15
  107.8 18.8 %collective-permute-start.14 = (bf16[512,256]{1,0:T(8,128)(2,1)S(1)}, bf16[512,256]{1,0:T(8,128)(2,1)S(1)}, u32[]{:S(2)}, u32[]{:S(2)}) collective-permute-start(bf16[512,256]{1,0:T(8,128)(2,1)S(1)} %pad_maximum_fusion.2), channel_id=1, source_target_pairs={{0,8},{8,16},{16,24},{24,32},{32,40},{40,48},{48,56},{56,64},{64,7... | collective-permute-start | bytes 786440 | tf_op jit(solution)/shard_map/ppermute | solution.py:15
  111.3 15.4 %collective-permute-start.15 = (bf16[512,256]{1,0:T(8,128)(2,1)S(1)}, bf16[512,256]{1,0:T(8,128)(2,1)S(1)}, u32[]{:S(2)}, u32[]{:S(2)}) collective-permute-start(bf16[512,256]{1,0:T(8,128)(2,1)S(1)} %pad_maximum_fusion.2), channel_id=1, source_target_pairs={{8,0},{16,8},{24,16},{32,24},{40,32},{48,40},{56,48},{64,56},{72,6... | collective-permute-start | bytes 786440 | tf_op jit(solution)/shard_map/ppermute | solution.py:15
  116.8 17.4 %collective-permute-start.16 = (bf16[512,256]{1,0:T(8,128)(2,1)S(1)}, bf16[512,256]{1,0:T(8,128)(2,1)S(1)}, u32[]{:S(2)}, u32[]{:S(2)}) collective-permute-start(bf16[512,256]{1,0:T(8,128)(2,1)S(1)} %pad_maximum_fusion.2), channel_id=1, source_target_pairs={{16,0},{24,8},{32,16},{40,24},{48,32},{56,40},{64,48},{72,56},{80,... | collective-permute-start | bytes 786440 | tf_op jit(solution)/shard_map/ppermute | solution.py:15
  120.2 15.6 %collective-permute-start.17 = (bf16[512,256]{1,0:T(8,128)(2,1)S(1)}, bf16[512,256]{1,0:T(8,128)(2,1)S(1)}, u32[]{:S(2)}, u32[]{:S(2)}) collective-permute-start(bf16[512,256]{1,0:T(8,128)(2,1)S(1)} %pad_maximum_fusion.2), channel_id=1, source_target_pairs={{24,0},{32,8},{40,16},{48,24},{56,32},{64,40},{72,48},{80,56},{88,... | collective-permute-start | bytes 786440 | tf_op jit(solution)/shard_map/ppermute | solution.py:15
  138.3 3.3 %copy-start.7 = (bf16[4,12,128,128]{3,2,1,0:T(8,128)(2,1)S(1)}, bf16[4,12,128,128]{3,2,1,0:T(8,128)(2,1)}, u32[]{:S(2)}) copy-start(bf16[4,12,128,128]{3,2,1,0:T(8,128)(2,1)} %param.14) | copy-start | bytes 4718596
  (3 other events, 8.6 us)
where the time goes:
time: 171 us; the launch traced here: 170 us
  starting transfers between devices  68 us (40%)
  blocking collectives  25.8 us (15%)
  waiting for transfers between devices  25.7 us (15%)
  local copies, waits for them, and re-layouts  24.2 us (14%)
  other arithmetic  13.6 us (8%)
  matrix products  10.9 us (6%)
  between operations  1.72 us (1%)
    ppermute x18, starting transfers between devices, from_behind(): lax.ppermute(value, axis, [(source, source + steps) for source in range(l...  68 us
    psum x1, blocking collectives, shards(): scen_total = lax.psum(local_sum, 'scen')  25.8 us
    ppermute x18, waiting for transfers between devices, from_behind(): lax.ppermute(value, axis, [(source, source + steps) for source in range(l...  25.7 us
    unnamed x33, local copies, waits for them, and re-layouts  10.6 us
    gather x3, local copies, waits for them, and re-layouts, shards(): gathered = jnp.take(nearby, window_index, axis=0)  10.5 us
    dot_general x3, matrix products, shards(): jnp.einsum('bsij,bsjk->bik', impedance_real, gathered, preferred_element_...  8.52 us
    scatter-add x1, other arithmetic, shards(): jax.ops.segment_sum(both_power, local_phase, num_segments=phase_count)  6.25 us
  transfers between devices with their start and end apart: 18, of which 5 were waited for; matrix products, arithmetic and copies ran while one was open for 7% of the time, Pallas kernels for 0%

commit v1 on v0

--- a/solution.py
+++ b/solution.py
@@ -83,7 +83,7 @@
         volt_imag = source_imag - drop_imag
     magnitude = jnp.sqrt(volt_real * volt_real + volt_imag * volt_imag)
     local_sum = jnp.sum(magnitude.reshape(phase_count, local_scen, TIMES), axis=1)
-    scen_total = lax.psum(local_sum, "scen")
+    scen_total = jnp.sum(lax.all_gather(local_sum, "scen"), axis=0)
     drop_mean = 100.0 * (1.0 - scen_total / total_scen)
     return (volt_real, volt_imag, drop_mean)
 

time: 171 us -> 160 us (0.936)
  the two profiles are of different devices: /device:TPU:224 before, /device:TPU:195 now
where the time goes in v1:
time: 160 us; the launch traced here: 159 us
  starting transfers between devices  61.1 us (38%)
  waiting for transfers between devices  31.8 us (20%)
  local copies, waits for them, and re-layouts  24.4 us (15%)
  blocking collectives  15.2 us (10%)
  other arithmetic  13.7 us (9%)
  matrix products  10.9 us (7%)
  between operations  1.73 us (1%)
    ppermute x18, starting transfers between devices, from_behind(): lax.ppermute(value, axis, [(source, source + steps) for source in range(l...  61.1 us
    ppermute x18, waiting for transfers between devices, from_behind(): lax.ppermute(value, axis, [(source, source + steps) for source in range(l...  31.8 us
    all_gather x1, blocking collectives, shards(): scen_total = jnp.sum(lax.all_gather(local_sum, 'scen'), axis=0)  15.2 us
    unnamed x34, local copies, waits for them, and re-layouts  10.7 us
    gather x3, local copies, waits for them, and re-layouts, shards(): gathered = jnp.take(nearby, window_index, axis=0)  10.5 us
    dot_general x3, matrix products, shards(): jnp.einsum('bsij,bsjk->bik', impedance_real, gathered, preferred_element_...  8.52 us
    scatter-add x1, other arithmetic, shards(): jax.ops.segment_sum(both_power, local_phase, num_segments=phase_count)  6.25 us
  transfers between devices with their start and end apart: 18, of which 6 were waited for; matrix products, arithmetic and copies ran while one was open for 8% of the time, Pallas kernels for 0%

profile of v1, /device:TPU:195, one launch (start us, length us, event | category | flops | bytes accessed | tf_op | source)
XLA Modules:
  0.0 158.8 jit_solution(6651124965556611296)
XLA Ops:
  3.6 6.2 %scatter_custom_fusion = f32[512,256]{1,0:T(8,128)S(1)} fusion(s32[1024]{0:T(1024)S(1)} %broadcast_subtract_fusion, f32[1024,128]{1,0:T(8,128)S(1)} %get-tuple-element.12, f32[]{:T(128)} %constant.112, f32[1024,128]{1,0:T(8,128)S(1)} %get-tuple-element.13, f32[]{:T(128)} %constant.78.clone.1), kind=kCustom, calls=%fused_computation.7 | custom fusion | flops 524288 | bytes 1572872 | tf_op jit(solution)/shard_map/scatter-add | solution.py:44
  10.2 3.5 %collective-permute-start = (bf16[512,256]{1,0:T(8,128)(2,1)S(1)}, bf16[512,256]{1,0:T(8,128)(2,1)}, u32[]{:S(2)}, u32[]{:S(2)}) collective-permute-start(bf16[512,256]{1,0:T(8,128)(2,1)S(1)} %pad_maximum_fusion), channel_id=1, source_target_pairs={{0,24},{8,32},{16,40},{24,48},{32,56},{40,64},{48,72},{56,80},{64,... | collective-permute-start | bytes 786440 | tf_op jit(solution)/shard_map/ppermute | solution.py:15
  13.7 4.0 %collective-permute-start.1 = (bf16[512,256]{1,0:T(8,128)(2,1)S(1)}, bf16[512,256]{1,0:T(8,128)(2,1)}, u32[]{:S(2)}, u32[]{:S(2)}) collective-permute-start(bf16[512,256]{1,0:T(8,128)(2,1)S(1)} %pad_maximum_fusion), channel_id=1, source_target_pairs={{0,16},{8,24},{16,32},{24,40},{32,48},{40,56},{48,64},{56,72},{64,... | collective-permute-start | bytes 786440 | tf_op jit(solution)/shard_map/ppermute | solution.py:15
  17.8 3.4 %collective-permute-start.2 = (bf16[512,256]{1,0:T(8,128)(2,1)S(1)}, bf16[512,256]{1,0:T(8,128)(2,1)S(1)}, u32[]{:S(2)}, u32[]{:S(2)}) collective-permute-start(bf16[512,256]{1,0:T(8,128)(2,1)S(1)} %pad_maximum_fusion), channel_id=1, source_target_pairs={{0,8},{8,16},{16,24},{24,32},{32,40},{40,48},{48,56},{56,64},{64,7... | collective-permute-start | bytes 786440 | tf_op jit(solution)/shard_map/ppermute | solution.py:15
  23.1 3.9 %collective-permute-start.4 = (bf16[512,256]{1,0:T(8,128)(2,1)S(1)}, bf16[512,256]{1,0:T(8,128)(2,1)S(1)}, u32[]{:S(2)}, u32[]{:S(2)}) collective-permute-start(bf16[512,256]{1,0:T(8,128)(2,1)S(1)} %pad_maximum_fusion), channel_id=1, source_target_pairs={{16,0},{24,8},{32,16},{40,24},{48,32},{56,40},{64,48},{72,56},{80,... | collective-permute-start | bytes 786440 | tf_op jit(solution)/shard_map/ppermute | solution.py:15
  29.7 3.5 %collective-permute-start.5 = (bf16[512,256]{1,0:T(8,128)(2,1)S(1)}, bf16[512,256]{1,0:T(8,128)(2,1)S(1)}, u32[]{:S(2)}, u32[]{:S(2)}) collective-permute-start(bf16[512,256]{1,0:T(8,128)(2,1)S(1)} %pad_maximum_fusion), channel_id=1, source_target_pairs={{24,0},{32,8},{40,16},{48,24},{56,32},{64,40},{72,48},{80,56},{88,... | collective-permute-start | bytes 786440 | tf_op jit(solution)/shard_map/ppermute | solution.py:15
  39.5 5.9 %collective-permute-done.5 = bf16[512,256]{1,0:T(8,128)(2,1)S(1)} collective-permute-done((bf16[512,256]{1,0:T(8,128)(2,1)S(1)}, bf16[512,256]{1,0:T(8,128)(2,1)S(1)}, u32[]{:S(2)}, u32[]{:S(2)}) %collective-permute-start.5) | collective-permute-done | bytes 262176 | tf_op jit(solution)/shard_map/ppermute | solution.py:15
  46.2 4.0 %gather_fusion = bf16[48,128,256]{2,1,0:T(8,128)(2,1)} fusion(bf16[28,128,256]{2,1,0:T(8,128)(2,1)} %bitcast.1, s32[1024]{0:T(1024)S(1)} %pad_clamp_fusion), kind=kCustom, calls=%fused_computation.clone | custom fusion | bytes 6291648 | tf_op jit(solution)/shard_map/jit(_take)/gather | solution.py:72
  50.2 2.8 %fusion.4 = f32[4,256,128,1]{1,2,3,0:T(8,128)S(1)} fusion(bf16[4,12,128,128]{3,2,1,0:T(8,128)(2,1)S(1)} %copy-done, bf16[4,12,128,256]{3,2,1,0:T(8,128)(2,1)} %bitcast.58, pred[12]{0:T(512)(128)(4,1)S(1)} %iota_compare_fusion, pred[4,12]{1,0:T(4,128)(4,1)S(1)} %get-tuple-element.10), kind=kOutput, calls=%fused_computation.11 | convolution fusion | flops 405798912 | bytes 5242940 | tf_op jit(solution)/shard_map/bsij,bsjk->bik/dot_general | solution.py:74
  57.4 3.7 %collective-permute-start.7 = (bf16[512,256]{1,0:T(8,128)(2,1)S(1)}, bf16[512,256]{1,0:T(8,128)(2,1)S(1)}, u32[]{:S(2)}, u32[]{:S(2)}) collective-permute-start(bf16[512,256]{1,0:T(8,128)(2,1)S(1)} %pad_maximum_fusion.1), channel_id=1, source_target_pairs={{0,16},{8,24},{16,32},{24,40},{32,48},{40,56},{48,64},{56,72},{64,... | collective-permute-start | bytes 786440 | tf_op jit(solution)/shard_map/ppermute | solution.py:15
  63.0 3.4 %collective-permute-start.9 = (bf16[512,256]{1,0:T(8,128)(2,1)S(1)}, bf16[512,256]{1,0:T(8,128)(2,1)S(1)}, u32[]{:S(2)}, u32[]{:S(2)}) collective-permute-start(bf16[512,256]{1,0:T(8,128)(2,1)S(1)} %pad_maximum_fusion.1), channel_id=1, source_target_pairs={{8,0},{16,8},{24,16},{32,24},{40,32},{48,40},{56,48},{64,56},{72,6... | collective-permute-start | bytes 786440 | tf_op jit(solution)/shard_map/ppermute | solution.py:15
  66.4 4.6 %collective-permute-start.10 = (bf16[512,256]{1,0:T(8,128)(2,1)S(1)}, bf16[512,256]{1,0:T(8,128)(2,1)S(1)}, u32[]{:S(2)}, u32[]{:S(2)}) collective-permute-start(bf16[512,256]{1,0:T(8,128)(2,1)S(1)} %pad_maximum_fusion.1), channel_id=1, source_target_pairs={{16,0},{24,8},{32,16},{40,24},{48,32},{56,40},{64,48},{72,56},{80,... | collective-permute-start | bytes 786440 | tf_op jit(solution)/shard_map/ppermute | solution.py:15
  71.0 4.0 %collective-permute-start.11 = (bf16[512,256]{1,0:T(8,128)(2,1)S(1)}, bf16[512,256]{1,0:T(8,128)(2,1)S(1)}, u32[]{:S(2)}, u32[]{:S(2)}) collective-permute-start(bf16[512,256]{1,0:T(8,128)(2,1)S(1)} %pad_maximum_fusion.1), channel_id=1, source_target_pairs={{24,0},{32,8},{40,16},{48,24},{56,32},{64,40},{72,48},{80,56},{88,... | collective-permute-start | bytes 786440 | tf_op jit(solution)/shard_map/ppermute | solution.py:15
  78.6 3.4 %collective-permute-done.10 = bf16[512,256]{1,0:T(8,128)(2,1)S(1)} collective-permute-done((bf16[512,256]{1,0:T(8,128)(2,1)S(1)}, bf16[512,256]{1,0:T(8,128)(2,1)S(1)}, u32[]{:S(2)}, u32[]{:S(2)}) %collective-permute-start.10) | collective-permute-done | bytes 262176 | tf_op jit(solution)/shard_map/ppermute | solution.py:15
  82.7 6.4 %collective-permute-done.11 = bf16[512,256]{1,0:T(8,128)(2,1)S(1)} collective-permute-done((bf16[512,256]{1,0:T(8,128)(2,1)S(1)}, bf16[512,256]{1,0:T(8,128)(2,1)S(1)}, u32[]{:S(2)}, u32[]{:S(2)}) %collective-permute-start.11) | collective-permute-done | bytes 262176 | tf_op jit(solution)/shard_map/ppermute | solution.py:15
  89.9 4.0 %gather_fusion.1 = bf16[48,128,256]{2,1,0:T(8,128)(2,1)} fusion(bf16[28,128,256]{2,1,0:T(8,128)(2,1)} %bitcast.15, s32[1024]{0:T(1024)S(1)} %pad_clamp_fusion), kind=kCustom, calls=%fused_computation.1.clone | custom fusion | bytes 6291648 | tf_op jit(solution)/shard_map/jit(_take)/gather | solution.py:72
  100.2 3.1 %collective-permute-start.13 = (bf16[512,256]{1,0:T(8,128)(2,1)S(1)}, bf16[512,256]{1,0:T(8,128)(2,1)S(1)}, u32[]{:S(2)}, u32[]{:S(2)}) collective-permute-start(bf16[512,256]{1,0:T(8,128)(2,1)S(1)} %pad_maximum_fusion.2), channel_id=1, source_target_pairs={{0,16},{8,24},{16,32},{24,40},{32,48},{40,56},{48,64},{56,72},{64,... | collective-permute-start | bytes 786440 | tf_op jit(solution)/shard_map/ppermute | solution.py:15
  105.8 3.7 %collective-permute-start.15 = (bf16[512,256]{1,0:T(8,128)(2,1)S(1)}, bf16[512,256]{1,0:T(8,128)(2,1)S(1)}, u32[]{:S(2)}, u32[]{:S(2)}) collective-permute-start(bf16[512,256]{1,0:T(8,128)(2,1)S(1)} %pad_maximum_fusion.2), channel_id=1, source_target_pairs={{8,0},{16,8},{24,16},{32,24},{40,32},{48,40},{56,48},{64,56},{72,6... | collective-permute-start | bytes 786440 | tf_op jit(solution)/shard_map/ppermute | solution.py:15
  109.5 4.6 %collective-permute-start.16 = (bf16[512,256]{1,0:T(8,128)(2,1)S(1)}, bf16[512,256]{1,0:T(8,128)(2,1)S(1)}, u32[]{:S(2)}, u32[]{:S(2)}) collective-permute-start(bf16[512,256]{1,0:T(8,128)(2,1)S(1)} %pad_maximum_fusion.2), channel_id=1, source_target_pairs={{16,0},{24,8},{32,16},{40,24},{48,32},{56,40},{64,48},{72,56},{80,... | collective-permute-start | bytes 786440 | tf_op jit(solution)/shard_map/ppermute | solution.py:15
  114.1 4.6 %collective-permute-start.17 = (bf16[512,256]{1,0:T(8,128)(2,1)S(1)}, bf16[512,256]{1,0:T(8,128)(2,1)S(1)}, u32[]{:S(2)}, u32[]{:S(2)}) collective-permute-start(bf16[512,256]{1,0:T(8,128)(2,1)S(1)} %pad_maximum_fusion.2), channel_id=1, source_target_pairs={{24,0},{32,8},{40,16},{48,24},{56,32},{64,40},{72,48},{80,56},{88,... | collective-permute-start | bytes 786440 | tf_op jit(solution)/shard_map/ppermute | solution.py:15
  118.8 5.6 %collective-permute-done.15 = bf16[512,256]{1,0:T(8,128)(2,1)S(1)} collective-permute-done((bf16[512,256]{1,0:T(8,128)(2,1)S(1)}, bf16[512,256]{1,0:T(8,128)(2,1)S(1)}, u32[]{:S(2)}, u32[]{:S(2)}) %collective-permute-start.15) | collective-permute-done | bytes 262176 | tf_op jit(solution)/shard_map/ppermute | solution.py:15
  124.5 3.5 %collective-permute-done.16 = bf16[512,256]{1,0:T(8,128)(2,1)S(1)} collective-permute-done((bf16[512,256]{1,0:T(8,128)(2,1)S(1)}, bf16[512,256]{1,0:T(8,128)(2,1)S(1)}, u32[]{:S(2)}, u32[]{:S(2)}) %collective-permute-start.16) | collective-permute-done | bytes 262176 | tf_op jit(solution)/shard_map/ppermute | solution.py:15
  128.1 6.9 %collective-permute-done.17 = bf16[512,256]{1,0:T(8,128)(2,1)S(1)} collective-permute-done((bf16[512,256]{1,0:T(8,128)(2,1)S(1)}, bf16[512,256]{1,0:T(8,128)(2,1)S(1)}, u32[]{:S(2)}, u32[]{:S(2)}) %collective-permute-start.17) | collective-permute-done | bytes 262176 | tf_op jit(solution)/shard_map/ppermute | solution.py:15
  142.7 15.2 %all-gather = f32[4096,16]{0,1:T(8,128)S(1)} all-gather(f32[512,16]{0,1:T(8,128)S(1)} %reduce_sum.28), channel_id=2, replica_groups=mesh['net'=64,'scen'=8] {'scen'}, dimensions={0}, use_global_device_ids=true | all-gather | bytes 294912 | tf_op jit(solution)/shard_map/all_gather | solution.py:86
  (85 shorter events, 43.0 us)
Async XLA Ops:
  0.6 49.6 %copy-start = (bf16[4,12,128,128]{3,2,1,0:T(8,128)(2,1)S(1)}, bf16[4,12,128,128]{3,2,1,0:T(8,128)(2,1)}, u32[]{:S(2)}) copy-start(bf16[4,12,128,128]{3,2,1,0:T(8,128)(2,1)} %param.13) | copy-start | bytes 4718596
  3.6 23.5 %copy-start.4 = (s32[4,12]{1,0:T(4,128)S(1)}, s32[4,12]{1,0:T(4,128)}, u32[]{:S(2)}) copy-start(s32[4,12]{1,0:T(4,128)} %param.12) | copy-start | bytes 580
  3.6 23.6 %copy-start.8 = (s32[64]{0:T(128)S(1)}, s32[64]{0:T(128)}, u32[]{:S(2)}) copy-start(s32[64]{0:T(128)} %param.11) | copy-start | bytes 772
  10.2 19.5 %collective-permute-start = (bf16[512,256]{1,0:T(8,128)(2,1)S(1)}, bf16[512,256]{1,0:T(8,128)(2,1)}, u32[]{:S(2)}, u32[]{:S(2)}) collective-permute-start(bf16[512,256]{1,0:T(8,128)(2,1)S(1)} %pad_maximum_fusion), channel_id=1, source_target_pairs={{0,24},{8,32},{16,40},{24,48},{32,56},{40,64},{48,72},{56,80},{64,... | collective-permute-start | bytes 786440 | tf_op jit(solution)/shard_map/ppermute | solution.py:15
  13.7 21.2 %collective-permute-start.1 = (bf16[512,256]{1,0:T(8,128)(2,1)S(1)}, bf16[512,256]{1,0:T(8,128)(2,1)}, u32[]{:S(2)}, u32[]{:S(2)}) collective-permute-start(bf16[512,256]{1,0:T(8,128)(2,1)S(1)} %pad_maximum_fusion), channel_id=1, source_target_pairs={{0,16},{8,24},{16,32},{24,40},{32,48},{40,56},{48,64},{56,72},{64,... | collective-permute-start | bytes 786440 | tf_op jit(solution)/shard_map/ppermute | solution.py:15
  17.8 18.8 %collective-permute-start.2 = (bf16[512,256]{1,0:T(8,128)(2,1)S(1)}, bf16[512,256]{1,0:T(8,128)(2,1)S(1)}, u32[]{:S(2)}, u32[]{:S(2)}) collective-permute-start(bf16[512,256]{1,0:T(8,128)(2,1)S(1)} %pad_maximum_fusion), channel_id=1, source_target_pairs={{0,8},{8,16},{16,24},{24,32},{32,40},{40,48},{48,56},{56,64},{64,7... | collective-permute-start | bytes 786440 | tf_op jit(solution)/shard_map/ppermute | solution.py:15
  21.2 16.8 %collective-permute-start.3 = (bf16[512,256]{1,0:T(8,128)(2,1)S(1)}, bf16[512,256]{1,0:T(8,128)(2,1)S(1)}, u32[]{:S(2)}, u32[]{:S(2)}) collective-permute-start(bf16[512,256]{1,0:T(8,128)(2,1)S(1)} %pad_maximum_fusion), channel_id=1, source_target_pairs={{8,0},{16,8},{24,16},{32,24},{40,32},{48,40},{56,48},{64,56},{72,6... | collective-permute-start | bytes 786440 | tf_op jit(solution)/shard_map/ppermute | solution.py:15
  23.1 15.7 %collective-permute-start.4 = (bf16[512,256]{1,0:T(8,128)(2,1)S(1)}, bf16[512,256]{1,0:T(8,128)(2,1)S(1)}, u32[]{:S(2)}, u32[]{:S(2)}) collective-permute-start(bf16[512,256]{1,0:T(8,128)(2,1)S(1)} %pad_maximum_fusion), channel_id=1, source_target_pairs={{16,0},{24,8},{32,16},{40,24},{48,32},{56,40},{64,48},{72,56},{80,... | collective-permute-start | bytes 786440 | tf_op jit(solution)/shard_map/ppermute | solution.py:15
  29.7 15.7 %collective-permute-start.5 = (bf16[512,256]{1,0:T(8,128)(2,1)S(1)}, bf16[512,256]{1,0:T(8,128)(2,1)S(1)}, u32[]{:S(2)}, u32[]{:S(2)}) collective-permute-start(bf16[512,256]{1,0:T(8,128)(2,1)S(1)} %pad_maximum_fusion), channel_id=1, source_target_pairs={{24,0},{32,8},{40,16},{48,24},{56,32},{64,40},{72,48},{80,56},{88,... | collective-permute-start | bytes 786440 | tf_op jit(solution)/shard_map/ppermute | solution.py:15
  50.2 3.3 %copy-start.5 = (bf16[4,12,128,128]{3,2,1,0:T(8,128)(2,1)S(1)}, bf16[4,12,128,128]{3,2,1,0:T(8,128)(2,1)}, u32[]{:S(2)}) copy-start(bf16[4,12,128,128]{3,2,1,0:T(8,128)(2,1)} %param.14) | copy-start | bytes 4718596
  54.6 16.4 %collective-permute-start.6 = (bf16[512,256]{1,0:T(8,128)(2,1)S(1)}, bf16[512,256]{1,0:T(8,128)(2,1)S(1)}, u32[]{:S(2)}, u32[]{:S(2)}) collective-permute-start(bf16[512,256]{1,0:T(8,128)(2,1)S(1)} %pad_maximum_fusion.1), channel_id=1, source_target_pairs={{0,24},{8,32},{16,40},{24,48},{32,56},{40,64},{48,72},{56,80},{64,... | collective-permute-start | bytes 786440 | tf_op jit(solution)/shard_map/ppermute | solution.py:15
  57.4 18.3 %collective-permute-start.7 = (bf16[512,256]{1,0:T(8,128)(2,1)S(1)}, bf16[512,256]{1,0:T(8,128)(2,1)S(1)}, u32[]{:S(2)}, u32[]{:S(2)}) collective-permute-start(bf16[512,256]{1,0:T(8,128)(2,1)S(1)} %pad_maximum_fusion.1), channel_id=1, source_target_pairs={{0,16},{8,24},{16,32},{24,40},{32,48},{40,56},{48,64},{56,72},{64,... | collective-permute-start | bytes 786440 | tf_op jit(solution)/shard_map/ppermute | solution.py:15
  61.1 15.3 %collective-permute-start.8 = (bf16[512,256]{1,0:T(8,128)(2,1)S(1)}, bf16[512,256]{1,0:T(8,128)(2,1)S(1)}, u32[]{:S(2)}, u32[]{:S(2)}) collective-permute-start(bf16[512,256]{1,0:T(8,128)(2,1)S(1)} %pad_maximum_fusion.1), channel_id=1, source_target_pairs={{0,8},{8,16},{16,24},{24,32},{32,40},{40,48},{48,56},{56,64},{64,7... | collective-permute-start | bytes 786440 | tf_op jit(solution)/shard_map/ppermute | solution.py:15
  63.0 14.9 %collective-permute-start.9 = (bf16[512,256]{1,0:T(8,128)(2,1)S(1)}, bf16[512,256]{1,0:T(8,128)(2,1)S(1)}, u32[]{:S(2)}, u32[]{:S(2)}) collective-permute-start(bf16[512,256]{1,0:T(8,128)(2,1)S(1)} %pad_maximum_fusion.1), channel_id=1, source_target_pairs={{8,0},{16,8},{24,16},{32,24},{40,32},{48,40},{56,48},{64,56},{72,6... | collective-permute-start | bytes 786440 | tf_op jit(solution)/shard_map/ppermute | solution.py:15
  66.4 15.6 %collective-permute-start.10 = (bf16[512,256]{1,0:T(8,128)(2,1)S(1)}, bf16[512,256]{1,0:T(8,128)(2,1)S(1)}, u32[]{:S(2)}, u32[]{:S(2)}) collective-permute-start(bf16[512,256]{1,0:T(8,128)(2,1)S(1)} %pad_maximum_fusion.1), channel_id=1, source_target_pairs={{16,0},{24,8},{32,16},{40,24},{48,32},{56,40},{64,48},{72,56},{80,... | collective-permute-start | bytes 786440 | tf_op jit(solution)/shard_map/ppermute | solution.py:15
  71.0 18.2 %collective-permute-start.11 = (bf16[512,256]{1,0:T(8,128)(2,1)S(1)}, bf16[512,256]{1,0:T(8,128)(2,1)S(1)}, u32[]{:S(2)}, u32[]{:S(2)}) collective-permute-start(bf16[512,256]{1,0:T(8,128)(2,1)S(1)} %pad_maximum_fusion.1), channel_id=1, source_target_pairs={{24,0},{32,8},{40,16},{48,24},{56,32},{64,40},{72,48},{80,56},{88,... | collective-permute-start | bytes 786440 | tf_op jit(solution)/shard_map/ppermute | solution.py:15
  93.9 3.3 %copy-start.6 = (bf16[4,12,128,128]{3,2,1,0:T(8,128)(2,1)S(1)}, bf16[4,12,128,128]{3,2,1,0:T(8,128)(2,1)}, u32[]{:S(2)}) copy-start(bf16[4,12,128,128]{3,2,1,0:T(8,128)(2,1)} %param.14) | copy-start | bytes 4718596
  98.3 15.8 %collective-permute-start.12 = (bf16[512,256]{1,0:T(8,128)(2,1)S(1)}, bf16[512,256]{1,0:T(8,128)(2,1)S(1)}, u32[]{:S(2)}, u32[]{:S(2)}) collective-permute-start(bf16[512,256]{1,0:T(8,128)(2,1)S(1)} %pad_maximum_fusion.2), channel_id=1, source_target_pairs={{0,24},{8,32},{16,40},{24,48},{32,56},{40,64},{48,72},{56,80},{64,... | collective-permute-start | bytes 786440 | tf_op jit(solution)/shard_map/ppermute | solution.py:15
  100.2 18.5 %collective-permute-start.13 = (bf16[512,256]{1,0:T(8,128)(2,1)S(1)}, bf16[512,256]{1,0:T(8,128)(2,1)S(1)}, u32[]{:S(2)}, u32[]{:S(2)}) collective-permute-start(bf16[512,256]{1,0:T(8,128)(2,1)S(1)} %pad_maximum_fusion.2), channel_id=1, source_target_pairs={{0,16},{8,24},{16,32},{24,40},{32,48},{40,56},{48,64},{56,72},{64,... | collective-permute-start | bytes 786440 | tf_op jit(solution)/shard_map/ppermute | solution.py:15
  103.3 15.5 %collective-permute-start.14 = (bf16[512,256]{1,0:T(8,128)(2,1)S(1)}, bf16[512,256]{1,0:T(8,128)(2,1)S(1)}, u32[]{:S(2)}, u32[]{:S(2)}) collective-permute-start(bf16[512,256]{1,0:T(8,128)(2,1)S(1)} %pad_maximum_fusion.2), channel_id=1, source_target_pairs={{0,8},{8,16},{16,24},{24,32},{32,40},{40,48},{48,56},{56,64},{64,7... | collective-permute-start | bytes 786440 | tf_op jit(solution)/shard_map/ppermute | solution.py:15
  105.8 18.7 %collective-permute-start.15 = (bf16[512,256]{1,0:T(8,128)(2,1)S(1)}, bf16[512,256]{1,0:T(8,128)(2,1)S(1)}, u32[]{:S(2)}, u32[]{:S(2)}) collective-permute-start(bf16[512,256]{1,0:T(8,128)(2,1)S(1)} %pad_maximum_fusion.2), channel_id=1, source_target_pairs={{8,0},{16,8},{24,16},{32,24},{40,32},{48,40},{56,48},{64,56},{72,6... | collective-permute-start | bytes 786440 | tf_op jit(solution)/shard_map/ppermute | solution.py:15
  109.5 18.6 %collective-permute-start.16 = (bf16[512,256]{1,0:T(8,128)(2,1)S(1)}, bf16[512,256]{1,0:T(8,128)(2,1)S(1)}, u32[]{:S(2)}, u32[]{:S(2)}) collective-permute-start(bf16[512,256]{1,0:T(8,128)(2,1)S(1)} %pad_maximum_fusion.2), channel_id=1, source_target_pairs={{16,0},{24,8},{32,16},{40,24},{48,32},{56,40},{64,48},{72,56},{80,... | collective-permute-start | bytes 786440 | tf_op jit(solution)/shard_map/ppermute | solution.py:15
  114.1 20.8 %collective-permute-start.17 = (bf16[512,256]{1,0:T(8,128)(2,1)S(1)}, bf16[512,256]{1,0:T(8,128)(2,1)S(1)}, u32[]{:S(2)}, u32[]{:S(2)}) collective-permute-start(bf16[512,256]{1,0:T(8,128)(2,1)S(1)} %pad_maximum_fusion.2), channel_id=1, source_target_pairs={{24,0},{32,8},{40,16},{48,24},{56,32},{64,40},{72,48},{80,56},{88,... | collective-permute-start | bytes 786440 | tf_op jit(solution)/shard_map/ppermute | solution.py:15
  137.4 3.3 %copy-start.7 = (bf16[4,12,128,128]{3,2,1,0:T(8,128)(2,1)S(1)}, bf16[4,12,128,128]{3,2,1,0:T(8,128)(2,1)}, u32[]{:S(2)}) copy-start(bf16[4,12,128,128]{3,2,1,0:T(8,128)(2,1)} %param.14) | copy-start | bytes 4718596
  (3 other events, 8.6 us)
